TPU v7x, 512 devices: a whole 4x8x8 slice. The times are simulated.
512 devices in a mesh: row: 32 (over y, x), col: 16 (over z, core).
Axes of the slice: x: 4, y: 8, z: 8, core: 2. Of those that a mesh axis runs over, the one named last changes fastest.
Arguments:
- noise: bfloat16 [4096, 16384], P('row', 'col'), as said below
- data: bfloat16 [4096, 16384], P('col', 'row'), may hold values from -5 to 5
Outputs:
- targets: bfloat16 [4096, 16384], P(('row', 'col'))
- noise_potential: float32 [4096], P('row')
- data_potential: float32 [4096], P('col')
Inputs may be any that keep to these rules, and one draw needn't show every extreme that they name: noise latents, real values of order one.
All inputs are finite; a program needn't handle non-finite values.
Results may differ from a plain program's by a relative error of at most 0.022.
Values may be sent and summed in bfloat16 or wider, within the bound.
A program may use at most 64 MiB of HBM per device.

v0:
```python
import math

import jax
import jax.numpy as jnp
from jax import lax
from jax.sharding import PartitionSpec as P

LATENT = 16384
ITERS = 3


def noise_update(cost_tile, data_pot, epsilon, log_count):
    scores = (data_pot[None, :] - cost_tile) / epsilon
    local_peak = jnp.max(scores, axis=1)
    highest = lax.pmax(local_peak, "col")
    summed = lax.psum(jnp.sum(jnp.exp(scores - highest[:, None]), axis=1), "col")
    return -epsilon * (log_count + highest + jnp.log(summed))


def data_update(cost_tile, noise_pot, epsilon, log_count):
    scores = (noise_pot[:, None] - cost_tile) / epsilon
    local_peak = jnp.max(scores, axis=0)
    highest = lax.pmax(local_peak, "row")
    summed = lax.psum(jnp.sum(jnp.exp(scores - highest[None, :]), axis=0), "row")
    return -epsilon * (log_count + highest + jnp.log(summed))


def per_device(noise, data):
    epsilon = 0.64 / math.sqrt(LATENT)
    contract = (((1,), (1,)), ((), ()))
    noise_full = lax.all_gather(noise, "col", axis=1, tiled=True)
    noise_norm = jnp.sum(jnp.square(noise_full.astype(jnp.float32)), axis=1) / LATENT
    noise_rows = noise.shape[0]
    data_rows = data.shape[0]
    data_full = lax.all_gather(data, "row", axis=1, tiled=True)
    data_norm = jnp.sum(jnp.square(data_full.astype(jnp.float32)), axis=1) / LATENT
    cross = lax.dot_general(noise_full, data_full, contract, preferred_element_type=jnp.float32)
    cost_tile = noise_norm[:, None] + data_norm[None, :] - 2.0 / LATENT * cross
    log_noise = math.log(noise_rows * lax.axis_size("row"))
    log_data = math.log(data_rows * lax.axis_size("col"))
    data_pot = jnp.zeros((data_rows,), jnp.float32)
    for step in range(ITERS):
        noise_pot = noise_update(cost_tile, data_pot, epsilon, log_noise)
        data_pot = data_update(cost_tile, noise_pot, epsilon, log_data)
    noise_pot = noise_update(cost_tile, data_pot, epsilon, log_noise)
    weights = jnp.exp(
        (noise_pot[:, None] + data_pot[None, :] - cost_tile) / epsilon + log_noise
    ).astype(jnp.bfloat16)
    targets = lax.psum_scatter(
        jnp.dot(weights, data_full, preferred_element_type=jnp.float32).astype(jnp.bfloat16),
        "col",
        scatter_dimension=0,
        tiled=True,
    )
    return (targets, noise_pot, data_pot)


def solution(mesh):
    placed = (P("row", "col"), P("col", "row"))
    return jax.shard_map(
        per_device,
        mesh=mesh,
        in_specs=placed,
        out_specs=(P(("row", "col"), None), P("row"), P("col")),
        check_vma=False,
    )
```

profile of v0, /device:TPU:2, one launch (start us, length us, event | category | flops | bytes accessed | tf_op | source)
XLA Modules:
  0.0 873.9 jit_solution(1578598648450638075)
XLA Ops:
  7.2 0.0 all-gather.3.cloned.1.call-start
  7.2 0.7 all-gather.3.cloned.1.call-update
  7.9 0.0 all-gather.5.cloned.1.call-start
  7.9 0.7 all-gather.5.cloned.1.call-update
  8.6 0.0 reduce-scatter.2.cloned.1.call-start
  8.7 51.8 %all-gather.3.cloned.1.call-done = bf16[128,16384]{1,0:T(8,128)(2,1)} async-done(((bf16[128,1024]{1,0:T(8,128)(2,1)}), bf16[128,16384]{1,0:T(8,128)(2,1)}) %all-gather.3.cloned.1.call-update) | async-done | bytes 4194320 | tf_op jit(solution)/shard_map/all_gather | solution.py:31
  60.5 3.1 multiply_reduce_fusion.1
  63.6 105.6 %all-gather.5.cloned.1.call-done = bf16[256,16384]{1,0:T(8,128)(2,1)} async-done(((bf16[256,512]{1,0:T(8,128)(2,1)}), bf16[256,16384]{1,0:T(8,128)(2,1)}) %all-gather.5.cloned.1.call-update) | async-done | bytes 8388624 | tf_op jit(solution)/shard_map/all_gather | solution.py:35
  169.2 0.0 copy-start
  169.2 5.3 multiply_reduce_fusion
  174.5 0.5 copy-done
  175.0 5.2 fusion.1
  180.2 24.2 %pmax.49 = f32[128]{0:T(128)S(1)} all-reduce(f32[128]{0:T(128)S(1)} %get-tuple-element.3), channel_id=1, replica_groups=mesh['row'=32,'col'=16] {'col'}, use_global_device_ids=true, to_apply=%region_3.0 | all-reduce | flops 128 | bytes 1024 | tf_op jit(solution)/shard_map/pmax | solution.py:15
  204.4 0.2 exponential_reduce_fusion.6
  204.5 23.9 %psum.49 = f32[128]{0:T(128)S(1)} all-reduce(f32[128]{0:T(128)S(1)} %exponential_reduce_fusion.6), channel_id=1, replica_groups=mesh['row'=32,'col'=16] {'col'}, use_global_device_ids=true, to_apply=%region_5.0 | all-reduce | flops 128 | bytes 1024 | tf_op jit(solution)/shard_map/psum | solution.py:16
  228.4 0.1 fusion.2
  228.5 71.5 %pmax.50 = f32[256]{0:T(256)S(1)} all-reduce(f32[256]{0:T(256)S(1)} %fusion.2), channel_id=1, replica_groups=mesh['row'=32,'col'=16] {'row'}, use_global_device_ids=true, to_apply=%region_7.0 | all-reduce | flops 256 | bytes 2048 | tf_op jit(solution)/shard_map/pmax | solution.py:23
  300.0 0.1 exponential_reduce_fusion.5
  300.2 73.0 %psum.50 = f32[256]{0:T(256)S(1)} all-reduce(f32[256]{0:T(256)S(1)} %exponential_reduce_fusion.5), channel_id=1, replica_groups=mesh['row'=32,'col'=16] {'row'}, use_global_device_ids=true, to_apply=%region_9.0 | all-reduce | flops 256 | bytes 2048 | tf_op jit(solution)/shard_map/psum | solution.py:24
  373.2 0.1 fusion.3
  373.3 23.5 %pmax.51 = f32[128]{0:T(128)S(1)} all-reduce(f32[128]{0:T(128)S(1)} %fusion.3), channel_id=1, replica_groups=mesh['row'=32,'col'=16] {'col'}, use_global_device_ids=true, to_apply=%region_11.0 | all-reduce | flops 128 | bytes 1024 | tf_op jit(solution)/shard_map/pmax | solution.py:15
  396.8 0.2 exponential_reduce_fusion.4
  397.0 23.5 %psum.51 = f32[128]{0:T(128)S(1)} all-reduce(f32[128]{0:T(128)S(1)} %exponential_reduce_fusion.4), channel_id=1, replica_groups=mesh['row'=32,'col'=16] {'col'}, use_global_device_ids=true, to_apply=%region_13.0 | all-reduce | flops 128 | bytes 1024 | tf_op jit(solution)/shard_map/psum | solution.py:16
  420.6 0.1 fusion.4
  420.7 69.6 %pmax.52 = f32[256]{0:T(256)S(1)} all-reduce(f32[256]{0:T(256)S(1)} %fusion.4), channel_id=1, replica_groups=mesh['row'=32,'col'=16] {'row'}, use_global_device_ids=true, to_apply=%region_15.0 | all-reduce | flops 256 | bytes 2048 | tf_op jit(solution)/shard_map/pmax | solution.py:23
  490.3 0.1 exponential_reduce_fusion.3
  490.4 71.6 %psum.52 = f32[256]{0:T(256)S(1)} all-reduce(f32[256]{0:T(256)S(1)} %exponential_reduce_fusion.3), channel_id=1, replica_groups=mesh['row'=32,'col'=16] {'row'}, use_global_device_ids=true, to_apply=%region_17.0 | all-reduce | flops 256 | bytes 2048 | tf_op jit(solution)/shard_map/psum | solution.py:24
  562.1 0.1 fusion.5
  562.2 23.5 %pmax.53 = f32[128]{0:T(128)S(1)} all-reduce(f32[128]{0:T(128)S(1)} %fusion.5), channel_id=1, replica_groups=mesh['row'=32,'col'=16] {'col'}, use_global_device_ids=true, to_apply=%region_19.0 | all-reduce | flops 128 | bytes 1024 | tf_op jit(solution)/shard_map/pmax | solution.py:15
  585.7 0.2 exponential_reduce_fusion.2
  585.9 23.5 %psum.53 = f32[128]{0:T(128)S(1)} all-reduce(f32[128]{0:T(128)S(1)} %exponential_reduce_fusion.2), channel_id=1, replica_groups=mesh['row'=32,'col'=16] {'col'}, use_global_device_ids=true, to_apply=%region_21.0 | all-reduce | flops 128 | bytes 1024 | tf_op jit(solution)/shard_map/psum | solution.py:16
  609.5 0.1 fusion.6
  609.6 69.6 %pmax.54 = f32[256]{0:T(256)S(1)} all-reduce(f32[256]{0:T(256)S(1)} %fusion.6), channel_id=1, replica_groups=mesh['row'=32,'col'=16] {'row'}, use_global_device_ids=true, to_apply=%region_23.0 | all-reduce | flops 256 | bytes 2048 | tf_op jit(solution)/shard_map/pmax | solution.py:23
  679.2 0.1 exponential_reduce_fusion.1
  679.3 71.6 %psum.54 = f32[256]{0:T(256)S(1)} all-reduce(f32[256]{0:T(256)S(1)} %exponential_reduce_fusion.1), channel_id=1, replica_groups=mesh['row'=32,'col'=16] {'row'}, use_global_device_ids=true, to_apply=%region_25.0 | all-reduce | flops 256 | bytes 2048 | tf_op jit(solution)/shard_map/psum | solution.py:24
  751.0 0.0 copy-start.1
  751.0 0.1 fusion.7
  751.1 23.5 %pmax.55 = f32[128]{0:T(128)S(1)} all-reduce(f32[128]{0:T(128)S(1)} %fusion.7), channel_id=1, replica_groups=mesh['row'=32,'col'=16] {'col'}, use_global_device_ids=true, to_apply=%region_27.0 | all-reduce | flops 128 | bytes 1024 | tf_op jit(solution)/shard_map/pmax | solution.py:15
  774.6 0.2 exponential_reduce_fusion
  774.8 23.5 %psum.55 = f32[128]{0:T(128)S(1)} all-reduce(f32[128]{0:T(128)S(1)} %exponential_reduce_fusion), channel_id=1, replica_groups=mesh['row'=32,'col'=16] {'col'}, use_global_device_ids=true, to_apply=%region_29.0 | all-reduce | flops 128 | bytes 1024 | tf_op jit(solution)/shard_map/psum | solution.py:16
  798.4 0.0 copy-start.2
  798.4 6.7 convolution_convert_fusion
  805.1 0.0 reduce-scatter.2.cloned.1.call-update
  805.1 0.0 copy-done.1
  805.1 0.0 copy-done.2
  805.1 62.3 %reduce-scatter.2.cloned.1.call-done = bf16[8,16384]{1,0:T(8,128)(2,1)} async-done(((bf16[128,16384]{1,0:T(8,128)(2,1)}), bf16[8,16384]{1,0:T(8,128)(2,1)}) %reduce-scatter.2.cloned.1.call-update) | async-done | bytes 262160 | tf_op jit(solution)/shard_map/reduce_scatter | solution.py:49
  (9 shorter events, 0.1 us)
Async XLA Ops:
  7.2 53.4 %all-gather.3.cloned.1.call-start = ((), (), s32[]{:S(2)}) async-start(), calls=%async_computation.1 | async-start | bytes 4456448 | tf_op jit(solution)/shard_map/all_gather | solution.py:31
  7.9 161.3 %all-gather.5.cloned.1.call-start = ((), (), s32[]{:S(2)}) async-start(), calls=%async_computation.2 | async-start | bytes 8650752 | tf_op jit(solution)/shard_map/all_gather | solution.py:35
  8.6 858.7 %reduce-scatter.2.cloned.1.call-start = ((), (), s32[]{:S(2)}) async-start(), calls=%async_computation.3 | async-start | bytes 4456448 | tf_op jit(solution)/shard_map/reduce_scatter | solution.py:49
  169.2 5.8 copy-start
  751.0 54.1 %copy-start.1 = (f32[256]{0:T(256)}, f32[256]{0:T(256)S(1)}, u32[]{:S(2)}) copy-start(f32[256]{0:T(256)S(1)} %add_multiply_fusion) | copy-start | bytes 3076
  798.4 6.7 copy-start.2
Sparse Core Ops, SparseCore 0:
  10.1 50.3 all-gather.2
  63.6 105.6 all-gather.4
  805.2 62.1 reduce-scatter.1
where the time goes:
time: 874 us
  blocking collectives  616 us (70%)
  waiting for transfers between devices  221 us (25%)
  between operations  13.8 us (2%)
  matrix products  11.9 us (1%)
  other arithmetic  10.2 us (1%)
    psum x3, blocking collectives, data_update(): lax.psum(jnp.sum(jnp.exp(scores - highest[None, :]), axis=0), 'row')  216 us
    pmax x3, blocking collectives, data_update(): highest = lax.pmax(local_peak, 'row')  211 us
    all_gather x1, waiting for transfers between devices, per_device(): data_full = lax.all_gather(data, 'row', axis=1, tiled=True)  106 us
    pmax x4, blocking collectives, noise_update(): highest = lax.pmax(local_peak, 'col')  94.8 us
    psum x4, blocking collectives, noise_update(): lax.psum(jnp.sum(jnp.exp(scores - highest[:, None]), axis=1), 'col')  94.5 us
    reduce_scatter x1, waiting for transfers between devices, per_device(): lax.psum_scatter(jnp.dot(weights, data_full, preferred_element_type=jnp.f...  62.3 us
    all_gather x1, waiting for transfers between devices, per_device(): noise_full = lax.all_gather(noise, 'col', axis=1, tiled=True)  51.8 us
  transfers between devices with their start and end apart: 3, of which 3 were waited for; matrix products, arithmetic and copies ran while one was open for 0% of the time, Pallas kernels for 0%

commit v1 on v0

v1 whole, which is shorter than its diff:
```python
import functools
import math

import jax
import jax.numpy as jnp
from jax import lax
from jax.experimental import pallas as pl
from jax.experimental.pallas import tpu as pltpu
from jax.sharding import PartitionSpec as P

LATENT = 16384
ITERS = 3
MESH = pl.DeviceIdType.MESH


def flip(line, copies):
    return jnp.transpose(jnp.broadcast_to(line, (copies, line.shape[1])))


def merge(slots_ref, step, log_count):
    peaks = slots_ref[step, :, 0, :]
    sums = slots_ref[step, :, 1, :]
    peak = jnp.max(peaks, axis=0, keepdims=True)
    total = jnp.sum(sums * jnp.exp(peaks - peak), axis=0, keepdims=True)
    return -(log_count + peak + jnp.log(total))


def sinkhorn_kernel(
    n_row, n_col, log_noise, log_data, cross_ref, data_norm_ref,
    weights_ref, u_ref, v_ref,
    score, score_t, f_slots, g_slots, f_send, f_recv, g_send, g_recv,
):
    row, col = lax.axis_index("row"), lax.axis_index("col")
    epsilon = 0.64 / math.sqrt(LATENT)

    def along_col(k):
        return (row, lax.rem(col + k, n_col))

    def along_row(k):
        return (lax.rem(row + k, n_row), col)

    barrier = pltpu.get_barrier_semaphore()

    @pl.loop(1, n_col)
    def _(k):
        pl.semaphore_signal(barrier, inc=1, device_id=along_col(k), device_id_type=MESH)

    @pl.loop(1, n_row)
    def _(k):
        pl.semaphore_signal(barrier, inc=1, device_id=along_row(k), device_id_type=MESH)

    score[...] = cross_ref[...] * (2.0 / LATENT / epsilon)
    score_t[...] = jnp.transpose(score[...])
    pl.semaphore_wait(barrier, n_col + n_row - 2)

    def exchange(scores, slots, step, count, target, send, recv):
        peak = jnp.max(scores, axis=0, keepdims=True)
        slots[step, 0, 0:1, :] = peak
        slots[step, 0, 1:2, :] = jnp.sum(jnp.exp(scores - peak), axis=0, keepdims=True)

        @pl.loop(1, count)
        def _(k):
            pltpu.make_async_remote_copy(
                src_ref=slots.at[step, 0], dst_ref=slots.at[step, k],
                send_sem=send.at[step], recv_sem=recv.at[step],
                device_id=target(k), device_id_type=MESH,
            ).start()

        others = slots.at[step, pl.ds(1, count - 1)]
        pltpu.make_async_copy(others, others, recv.at[step]).wait()

    def drain(slots, step, count, send):
        others = slots.at[step, pl.ds(1, count - 1)]
        pltpu.make_async_copy(others, others, send.at[step]).wait()

    def noise_update(step, v):
        scores = score_t[...] + flip(v, score_t.shape[1])
        exchange(scores, f_slots, step, n_col, along_col, f_send, f_recv)
        return merge(f_slots, step, log_data)

    def data_update(step, u):
        rows = flip(u, 128)
        scores = score[...] + jnp.concatenate([rows] * (score.shape[1] // 128), axis=1)
        exchange(scores, g_slots, step, n_row, along_row, g_send, g_recv)
        return merge(g_slots, step, log_noise)

    v = -data_norm_ref[...] / epsilon
    for step in range(ITERS):
        u = noise_update(step, v)
        v = data_update(step, u)
    u = noise_update(ITERS, v)
    u_ref[...] = u
    v_ref[...] = v
    rows = flip(u, 128)
    rows = jnp.concatenate([rows] * (score.shape[1] // 128), axis=1)
    weights_ref[...] = jnp.exp(score[...] + rows + v + log_noise).astype(jnp.bfloat16)
    for step in range(ITERS + 1):
        drain(f_slots, step, n_col, f_send)
    for step in range(ITERS):
        drain(g_slots, step, n_row, g_send)


def per_device(noise, data):
    n_row, n_col = lax.axis_size("row"), lax.axis_size("col")
    epsilon = 0.64 / math.sqrt(LATENT)
    contract = (((1,), (1,)), ((), ()))
    noise_full = lax.all_gather(noise, "col", axis=1, tiled=True)
    noise_norm = jnp.sum(jnp.square(noise_full.astype(jnp.float32)), axis=1) / LATENT
    rows, cols = noise.shape[0], data.shape[0]
    data_full = lax.all_gather(data, "row", axis=1, tiled=True)
    data_norm = jnp.sum(jnp.square(data_full.astype(jnp.float32)), axis=1) / LATENT
    cross = lax.dot_general(noise_full, data_full, contract, preferred_element_type=jnp.float32)
    vmem = pl.BlockSpec(memory_space=pltpu.VMEM)
    dma = pltpu.SemaphoreType.DMA
    weights, u, v = pl.pallas_call(
        functools.partial(
            sinkhorn_kernel, n_row, n_col, math.log(rows * n_row), math.log(cols * n_col)
        ),
        out_shape=(
            jax.ShapeDtypeStruct((rows, cols), jnp.bfloat16),
            jax.ShapeDtypeStruct((1, rows), jnp.float32),
            jax.ShapeDtypeStruct((1, cols), jnp.float32),
        ),
        in_specs=[vmem, vmem],
        out_specs=(vmem, vmem, vmem),
        scratch_shapes=[
            pltpu.VMEM((rows, cols), jnp.float32),
            pltpu.VMEM((cols, rows), jnp.float32),
            pltpu.VMEM((ITERS + 1, n_col, 2, rows), jnp.float32),
            pltpu.VMEM((ITERS, n_row, 2, cols), jnp.float32),
            dma((ITERS + 1,)), dma((ITERS + 1,)), dma((ITERS,)), dma((ITERS,)),
        ],
        compiler_params=pltpu.CompilerParams(
            collective_id=0, has_side_effects=True, vmem_limit_bytes=16 * 2**20
        ),
        name="sinkhorn",
    )(cross, data_norm[None, :])
    noise_pot = epsilon * u[0] + noise_norm
    data_pot = epsilon * v[0] + data_norm
    targets = lax.psum_scatter(
        jnp.dot(weights, data_full, preferred_element_type=jnp.float32).astype(jnp.bfloat16),
        "col",
        scatter_dimension=0,
        tiled=True,
    )
    return (targets, noise_pot, data_pot)


def solution(mesh):
    placed = (P("row", "col"), P("col", "row"))
    return jax.shard_map(
        per_device,
        mesh=mesh,
        in_specs=placed,
        out_specs=(P(("row", "col"), None), P("row"), P("col")),
        check_vma=False,
    )
```

time: 874 us -> 297 us (0.34)
  the two profiles are of different devices: /device:TPU:2 before, /device:TPU:8 now
where the time goes in v1:
time: 297 us
  waiting for transfers between devices  217 us (73%)
  Pallas kernels  45.4 us (15%)
  between operations  13.8 us (5%)
  matrix products  10.9 us (4%)
  other arithmetic  9.32 us (3%)
    all_gather x1, waiting for transfers between devices, per_device(): data_full = lax.all_gather(data, 'row', axis=1, tiled=True)  116 us
    reduce_scatter x1, waiting for transfers between devices, per_device(): lax.psum_scatter(jnp.dot(weights, data_full, preferred_element_type=jnp.f...  59.3 us
    pallas_call x1, Pallas kernels, per_device(): pl.pallas_call(functools.partial(sinkhorn_kernel, n_row, n_col, math.log(...  45.4 us
    all_gather x1, waiting for transfers between devices, per_device(): noise_full = lax.all_gather(noise, 'col', axis=1, tiled=True)  40.8 us
    dot_general x1, matrix products, per_device(): lax.dot_general(noise_full, data_full, contract, preferred_element_type=j...  7.71 us
  transfers between devices with their start and end apart: 3, of which 3 were waited for; matrix products, arithmetic and copies ran while one was open for 3% of the time, Pallas kernels for 0%

profile of v1, /device:TPU:8, one launch (start us, length us, event | category | flops | bytes accessed | tf_op | source)
XLA Modules:
  0.0 296.9 jit_solution(3164669276346434789)
XLA Ops:
  7.2 0.0 all-gather.5.cloned.1.call-start
  7.2 0.7 all-gather.5.cloned.1.call-update
  7.9 0.0 all-gather.3.cloned.1.call-start
  7.9 0.7 all-gather.3.cloned.1.call-update
  8.6 0.0 reduce-scatter.2.cloned.1.call-start
  8.7 115.8 %all-gather.5.cloned.1.call-done = bf16[256,16384]{1,0:T(8,128)(2,1)} async-done(((bf16[256,512]{1,0:T(8,128)(2,1)}), bf16[256,16384]{1,0:T(8,128)(2,1)}) %all-gather.5.cloned.1.call-update) | async-done | bytes 8388624 | tf_op jit(solution)/shard_map/all_gather | solution.py:110
  124.5 5.1 %multiply_reduce_fusion = f32[256]{0:T(256)S(1)} fusion(bf16[256,16384]{1,0:T(8,128)(2,1)} %all-gather.5.cloned.1.call-done), kind=kLoop, calls=%fused_computation.1 | loop fusion | flops 12582656 | bytes 8389632 | tf_op jit(solution)/shard_map/reduce_sum | solution.py:111
  129.7 40.8 %all-gather.3.cloned.1.call-done = bf16[128,16384]{1,0:T(8,128)(2,1)} async-done(((bf16[128,1024]{1,0:T(8,128)(2,1)}), bf16[128,16384]{1,0:T(8,128)(2,1)}) %all-gather.3.cloned.1.call-update) | async-done | bytes 4194320 | tf_op jit(solution)/shard_map/all_gather | solution.py:107
  170.4 0.0 copy-start
  170.5 7.7 %fusion.1.cross_ref = f32[128,256]{1,0:T(8,128)S(1)} fusion(bf16[128,16384]{1,0:T(8,128)(2,1)} %all-gather.3.cloned.1.call-done, bf16[256,16384]{1,0:T(8,128)(2,1)} %all-gather.5.cloned.1.call-done), kind=kOutput, calls=%fused_computation.7 | convolution fusion | flops 1073741824 | bytes 12713984 | tf_op jit(solution)/shard_map/dot_general | solution.py:112
  178.2 45.4 %sinkhorn.1 = (bf16[128,256]{1,0:T(8,128)(2,1)S(1)}, f32[1,128]{1,0:T(1,128)S(1)}, f32[1,256]{1,0:T(1,128)S(1)}) custom-call(f32[128,256]{1,0:T(8,128)S(1)} %fusion.1.cross_ref, f32[1,256]{1,0:T(1,128)S(1)} %bitcast.8), custom_call_target="tpu_custom_call" | custom-call | tf_op jit(solution)/shard_map/sinkhorn/pallas_call | solution.py:115
  223.6 0.0 copy-done
  223.6 3.2 %convolution_convert_fusion = bf16[128,16384]{1,0:T(8,128)(2,1)} fusion(bf16[128,256]{1,0:T(8,128)(2,1)S(1)} %get-tuple-element.6, bf16[256,16384]{1,0:T(8,128)(2,1)S(1)} %copy-done), kind=kOutput, calls=%fused_computation | convolution fusion | flops 1075838976 | bytes 12648448 | tf_op jit(solution)/shard_map/dot_general | solution.py:141
  226.8 0.0 reduce-scatter.2.cloned.1.call-update
  226.8 3.1 %multiply_reduce_fusion.1 = f32[128]{0:T(128)S(1)} fusion(bf16[128,16384]{1,0:T(8,128)(2,1)} %all-gather.3.cloned.1.call-done), kind=kLoop, calls=%fused_computation.2 | loop fusion | flops 6291328 | bytes 4194816 | tf_op jit(solution)/shard_map/reduce_sum | solution.py:108
  229.9 0.5 bitcast_add_fusion
  230.4 0.6 fusion
  231.0 59.3 %reduce-scatter.2.cloned.1.call-done = bf16[8,16384]{1,0:T(8,128)(2,1)} async-done(((bf16[128,16384]{1,0:T(8,128)(2,1)}), bf16[8,16384]{1,0:T(8,128)(2,1)}) %reduce-scatter.2.cloned.1.call-update) | async-done | bytes 262160 | tf_op jit(solution)/shard_map/reduce_scatter | solution.py:140
  (2 shorter events, 0.0 us)
Async XLA Ops:
  7.2 117.3 %all-gather.5.cloned.1.call-start = ((), (), s32[]{:S(2)}) async-start(), calls=%async_computation.2 | async-start | bytes 8650752 | tf_op jit(solution)/shard_map/all_gather | solution.py:110
  7.9 162.6 %all-gather.3.cloned.1.call-start = ((), (), s32[]{:S(2)}) async-start(), calls=%async_computation.1 | async-start | bytes 4456448 | tf_op jit(solution)/shard_map/all_gather | solution.py:107
  8.6 281.7 %reduce-scatter.2.cloned.1.call-start = ((), (), s32[]{:S(2)}) async-start(), calls=%async_computation.3 | async-start | bytes 4456448 | tf_op jit(solution)/shard_map/reduce_scatter | solution.py:140
  170.4 53.1 %copy-start = (bf16[256,16384]{1,0:T(8,128)(2,1)S(1)}, bf16[256,16384]{1,0:T(8,128)(2,1)}, u32[]{:S(2)}) copy-start(bf16[256,16384]{1,0:T(8,128)(2,1)} %all-gather.5.cloned.1.call-done) | copy-start | bytes 25165828
Sparse Core Ops, SparseCore 0:
  11.0 113.4 all-gather.4
  126.7 43.7 all-gather.2
  227.0 63.3 reduce-scatter.1

commit v2 on v0

v2 whole, which is shorter than its diff:
```python
import math

import jax
import jax.numpy as jnp
from jax import lax
from jax.experimental import pallas as pl
from jax.experimental.pallas import tpu as pltpu
from jax.sharding import PartitionSpec as P

LATENT = 16384
ITERS = 3
X, Y, Z = 4, 8, 8
N_ROW, N_COL = X * Y, 2 * Z
ROWS, COLS = 128, 256
LOG_COUNT = math.log(4096)
EPSILON = 0.64 / math.sqrt(LATENT)
BLOCK = 512
MESH = pl.DeviceIdType.MESH
F32, BF16 = jnp.float32, jnp.bfloat16


def flip(line, copies):
    return jnp.transpose(jnp.broadcast_to(line, (copies, line.shape[1])))


def squares(block):
    block = jnp.square(block.astype(F32))
    return sum(block[:, i : i + 128] for i in range(0, block.shape[1], 128))


def hops(way, half):
    return 4 if way == half else 3


def kernel(
    noise_ref, data_ref, out_ref, noise_pot_ref, data_pot_ref,
    nb, dd, part, part_in, square_sum, norm_slots, score, score_t, f_slots, g_slots,
    w_send, w_all, po, rs_in, rs_out, fin_send, fin_in,
    own_send, own_recv, ring_send, ring_recv, pair_send, pair_recv, dpair_send, dpair_recv,
    part_s, part_r, norm_s, norm_r, f_send, f_recv, g_send, g_recv, w_s, w_r,
    rs_s, rs_r, fin_s, fin_r,
):
    row, col = lax.axis_index("row"), lax.axis_index("col")
    y, x = row // X, lax.rem(row, X)
    z, c = col // 2, lax.rem(col, 2)
    other = 1 - c

    def at(y_, x_, z_, c_):
        return (y_ * X + x_, z_ * 2 + c_)

    def wrap(i, n):
        return lax.rem(i + n, n)

    def send(src, dst, send_sem, recv_sem, device):
        return pltpu.make_async_remote_copy(
            src_ref=src, dst_ref=dst, send_sem=send_sem, recv_sem=recv_sem,
            device_id=device, device_id_type=MESH,
        )

    def take(ref, sem):
        pltpu.make_async_copy(ref, ref, sem).wait()

    barrier = pltpu.get_barrier_semaphore()
    near = [at(wrap(y + 1, Y), x, z, c), at(wrap(y - 1, Y), x, z, c)]
    near += [at(y, x, wrap(z + 1, Z), c), at(y, x, wrap(z - 1, Z), c), at(y, x, z, other)]
    for k in range(1, X):
        near += [at(y, wrap(x + k, X), z, c), at(y, wrap(x + k, X), z, other)]
    for device in near:
        pl.semaphore_signal(barrier, inc=1, device_id=device, device_id_type=MESH)
    dd[c, y] = data_ref[...]
    pl.semaphore_wait(barrier, len(near))

    def ring(kind, way, half, step):
        place = (y, z)[kind]
        sign = 1 - 2 * way
        block = wrap(place - sign * (step - 1), 8)
        target = wrap(place + sign, 8)
        if kind == 0:
            ref = dd.at[c, block, pl.ds(half * 128, 128)]
            device = at(target, x, z, c)
        else:
            ref = nb.at[block, pl.ds(pl.multiple_of(c * 256 + half * 128, 128), 128)]
            device = at(y, x, target, c)
        index = (kind, way, half, step - 1)
        return send(ref, ref, ring_send.at[index], ring_recv.at[index], device)

    for half in range(2):
        for way in range(2):
            ring(0, way, half, 1).start()

    mine = x // 2 == c
    n1_device = [at(y, 2 * c + h, z, x // 2) for h in range(2)]
    n1_self = [jnp.logical_and(mine, lax.rem(x, 2) == h) for h in range(2)]
    n1_dst = nb.at[z, pl.ds(pl.multiple_of(x * ROWS, ROWS), ROWS)]
    n1_sem = own_recv.at[lax.rem(x, 2)]
    n1 = []
    for h in range(2):
        src = noise_ref.at[:, pl.ds(h * BLOCK, BLOCK)]
        far = send(src, n1_dst, own_send.at[h], n1_sem, n1_device[h])
        near_copy = pltpu.make_async_copy(src, n1_dst, n1_sem)
        n1.append(far)

        @pl.when(n1_self[h])
        def _():
            near_copy.start()

        @pl.when(jnp.logical_not(n1_self[h]))
        def _():
            far.start()

    def half_of(block, core, half):
        return nb.at[block, pl.ds(pl.multiple_of(core * 256 + half * 128, 128), 128)]

    def pair(way, half, step, block):
        index = (way, half, step)
        ref = half_of(block, c, half)
        return send(ref, ref, pair_send.at[index], pair_recv.at[index], at(y, x, z, other))

    pairs = []
    for half in range(2):
        take(half_of(z, c, half), own_recv.at[half])
        for way in range(2):
            ring(1, way, half, 1).start()
        pairs.append(pair(0, half, 0, z))
        pairs[-1].start()

    square_sum[...] = squares(data_ref[...])
    for step in range(1, 5):
        for kind in range(2):
            for half in range(2):
                for way in range(2):
                    if step > hops(way, half):
                        continue
                    arrived = ring(kind, way, half, step)
                    arrived.wait_recv()
                    if step < hops(way, half):
                        ring(kind, way, half, step + 1).start()
                    if kind == 1:
                        block = wrap(z - (1 - 2 * way) * step, Z)
                        pairs.append(pair(way, half, step, block))
                        pairs[-1].start()
        if step < 4:
            for block in (wrap(y - step, Y), wrap(y + step, Y)):
                square_sum[...] += squares(dd[c, block])
    for copy in pairs:
        copy.wait_recv()

    part[...] = jnp.zeros_like(part)

    @pl.loop(0, Y)
    def _(k):
        part[...] += lax.dot_general(
            nb[k], dd[c, k], (((1,), (1,)), ((), ())), preferred_element_type=F32
        )

    part_copies = []
    for k in (2, 1, 3):
        target = wrap(x + k, X)
        copy = send(
            part.at[pl.ds(pl.multiple_of(target * ROWS, ROWS), ROWS)], part_in.at[k - 1],
            part_s.at[k - 1], part_r.at[k - 1], at(y, target, z, c),
        )
        copy.start()
        part_copies.append(copy)
    square_sum[...] += squares(dd[c, wrap(y + 4, Y)])
    norm_slots[x] = jnp.sum(jnp.transpose(square_sum[...]), axis=0, keepdims=True)
    for k in range(1, X):
        send(
            norm_slots.at[x], norm_slots.at[x], norm_s, norm_r, at(y, wrap(x + k, X), z, c)
        ).start()
    fold = squares(noise_ref[...])
    noise_squares = jnp.sum(jnp.transpose(fold), axis=0, keepdims=True)
    for copy in part_copies:
        copy.wait_recv()
    total = part[pl.ds(pl.multiple_of(x * ROWS, ROWS), ROWS), :]
    total = total + part_in[0] + part_in[1] + part_in[2]
    score[...] = total * (2.0 / LATENT / EPSILON)
    score_t[...] = jnp.transpose(score[...])
    take(norm_slots.at[pl.ds(0, X - 1)], norm_r)
    data_norm = (norm_slots[0] + norm_slots[1] + norm_slots[2] + norm_slots[3]) / LATENT

    dpair = send(dd.at[c], dd.at[c], dpair_send, dpair_recv, at(y, x, z, other))
    dpair.start()

    def along_col(k):
        return (row, lax.rem(col + k, N_COL))

    def along_row(k):
        return (lax.rem(row + k, N_ROW), col)

    def exchange(scores, slots, step, me, count, target, send_sem, recv_sem):
        peak = jnp.max(scores, axis=0, keepdims=True)
        slots[step, me, 0:1, :] = peak
        slots[step, me, 1:2, :] = jnp.sum(jnp.exp(scores - peak), axis=0, keepdims=True)

        @pl.loop(1, count)
        def _(k):
            ref = slots.at[step, me]
            send(ref, ref, send_sem.at[step], recv_sem.at[step], target(k)).start()

        take(slots.at[step, pl.ds(0, count - 1)], recv_sem.at[step])
        peaks, sums = slots[step, :, 0, :], slots[step, :, 1, :]
        peak = jnp.max(peaks, axis=0, keepdims=True)
        total = jnp.sum(sums * jnp.exp(peaks - peak), axis=0, keepdims=True)
        return -(LOG_COUNT + peak + jnp.log(total))

    def wide(u):
        tile = flip(u, 128)
        return jnp.concatenate([tile] * (COLS // 128), axis=1)

    def noise_update(step, v):
        f_slots[step, col, 2:3, :] = noise_squares
        scores = score_t[...] + flip(v, ROWS)
        return exchange(scores, f_slots, step, col, N_COL, along_col, f_send, f_recv)

    def data_update(step, u):
        scores = score[...] + wide(u)
        return exchange(scores, g_slots, step, row, N_ROW, along_row, g_send, g_recv)

    v = -data_norm / EPSILON
    for step in range(ITERS):
        u = noise_update(step, v)
        v = data_update(step, u)
    u = noise_update(ITERS, v)

    weights = jnp.exp(score[...] + wide(u) + v + LOG_COUNT).reshape(Z, 2, 8, COLS)
    for core in range(2):
        w_send[core] = weights[:, core].reshape(Z * 8, COLS).astype(BF16)
    for k in range(X):
        for flipped in range(2):
            if k == 0 and flipped == 0:
                continue
            core = wrap(c + flipped, 2)
            send(
                w_send.at[core], w_all.at[c * X + x], w_s, w_r, at(y, wrap(x + k, X), z, core)
            ).start()
    w_all[c * X + x] = w_send[c]
    noise_norm = jnp.sum(f_slots[0, :, 2, :], axis=0, keepdims=True) / LATENT
    noise_pot_ref[...] = EPSILON * u + noise_norm
    data_pot_ref[...] = EPSILON * v + data_norm
    dpair.wait_recv()
    take(w_all.at[pl.ds(0, 2 * X - 1)], w_r)

    def rs(way, half, step):
        sign = 1 - 2 * way
        index = (way, half, step - 1)
        if step == 1:
            src = po.at[half, wrap(z + sign * hops(way, half), Z)]
        else:
            src = rs_out.at[way, half, step - 2]
        return send(
            src, rs_in.at[index], rs_s.at[index], rs_r.at[index], at(y, x, wrap(z + sign, Z), c)
        )

    for half in range(2):
        @pl.loop(0, Y // 2)
        def _(j):
            block = half * (Y // 2) + j
            sums = jnp.dot(
                w_all[0:X].reshape(256, COLS), dd[0, block], preferred_element_type=F32
            ) + jnp.dot(w_all[X:].reshape(256, COLS), dd[1, block], preferred_element_type=F32)
            sums = sums.reshape(X, Z, 8, BLOCK)
            columns = pl.ds(pl.multiple_of(j * BLOCK, BLOCK), BLOCK)
            for k in range(Z):
                po[half, k, :, columns] = sums[:, k].reshape(X * 8, BLOCK).astype(BF16)

        for way in range(2):
            rs(way, half, 1).start()

    for step in range(1, 5):
        for half in range(2):
            for way in range(2):
                if step > hops(way, half):
                    continue
                rs(way, half, step).wait_recv()
                if step < hops(way, half):
                    target = wrap(z + (1 - 2 * way) * (hops(way, half) - step), Z)
                    rs_out[way, half, step - 1] = (
                        rs_in[way, half, step - 1].astype(F32) + po[half, target].astype(F32)
                    ).astype(BF16)
                    rs(way, half, step + 1).start()
    for half in range(2):
        sums = po[half, z].astype(F32)
        for way in range(2):
            sums = sums + rs_in[way, half, hops(way, half) - 1].astype(F32)
        for k in range(X):
            lines = sums[k * 8 : k * 8 + 8]
            lines = jnp.concatenate([lines[:, :1024], lines[:, 1024:]], axis=0)
            fin_send[half, k] = lines.astype(BF16)
        fin_in[half, x] = fin_send[half, x]
        for k in range(1, X):
            target = wrap(x + k, X)
            send(
                fin_send.at[half, target], fin_in.at[half, x], fin_s.at[half], fin_r.at[half],
                at(y, target, z, c),
            ).start()
    for half in range(2):
        take(fin_in.at[half, pl.ds(0, X - 1)], fin_r.at[half])
        for k in range(X):
            lines = fin_in[half, k].astype(F32)
            for quarter in range(2):
                for part_block in range(2):
                    block = half * 4 + quarter * 2 + part_block
                    begin = (block * X + k) * BLOCK
                    out_ref[:, begin : begin + BLOCK] = lines[
                        quarter * 8 : quarter * 8 + 8, part_block * BLOCK : (part_block + 1) * BLOCK
                    ].astype(BF16)

    for h in range(2):
        @pl.when(jnp.logical_not(n1_self[h]))
        def _():
            n1[h].wait_send()
    for kind in range(2):
        for half in range(2):
            for way in range(2):
                for step in range(1, hops(way, half) + 1):
                    ring(kind, way, half, step).wait_send()
                    if kind == 0:
                        rs(way, half, step).wait_send()
    for copy in pairs + part_copies + [dpair]:
        copy.wait_send()
    take(norm_slots.at[pl.ds(0, X - 1)], norm_s)
    take(w_all.at[pl.ds(0, 2 * X - 1)], w_s)
    for half in range(2):
        take(fin_in.at[half, pl.ds(0, X - 1)], fin_s.at[half])
    for step in range(ITERS + 1):
        take(f_slots.at[step, pl.ds(0, N_COL - 1)], f_send.at[step])
    for step in range(ITERS):
        take(g_slots.at[step, pl.ds(0, N_ROW - 1)], g_send.at[step])


def per_device(noise, data):
    vmem = pl.BlockSpec(memory_space=pltpu.VMEM)
    dma = pltpu.SemaphoreType.DMA
    targets, noise_pot, data_pot = pl.pallas_call(
        kernel,
        out_shape=(
            jax.ShapeDtypeStruct((8, LATENT), BF16),
            jax.ShapeDtypeStruct((1, ROWS), F32),
            jax.ShapeDtypeStruct((1, COLS), F32),
        ),
        in_specs=[vmem, vmem],
        out_specs=(vmem, vmem, vmem),
        scratch_shapes=[
            pltpu.VMEM((Z, X * ROWS, BLOCK), BF16),
            pltpu.VMEM((2, Y, COLS, BLOCK), BF16),
            pltpu.VMEM((X * ROWS, COLS), F32),
            pltpu.VMEM((X - 1, ROWS, COLS), F32),
            pltpu.VMEM((COLS, 128), F32),
            pltpu.VMEM((X, 1, COLS), F32),
            pltpu.VMEM((ROWS, COLS), F32),
            pltpu.VMEM((COLS, ROWS), F32),
            pltpu.VMEM((ITERS + 1, N_COL, 3, ROWS), F32),
            pltpu.VMEM((ITERS, N_ROW, 2, COLS), F32),
            pltpu.VMEM((2, Z * 8, COLS), BF16),
            pltpu.VMEM((2 * X, Z * 8, COLS), BF16),
            pltpu.VMEM((2, Z, X * 8, 2048), BF16),
            pltpu.VMEM((2, 2, 4, X * 8, 2048), BF16),
            pltpu.VMEM((2, 2, 3, X * 8, 2048), BF16),
            pltpu.VMEM((2, X, 16, 1024), BF16),
            pltpu.VMEM((2, X, 16, 1024), BF16),
            dma((2,)), dma((2,)), dma((2, 2, 2, 4)), dma((2, 2, 2, 4)),
            dma((2, 2, 5)), dma((2, 2, 5)), dma, dma,
            dma((3,)), dma((3,)), dma, dma,
            dma((ITERS + 1,)), dma((ITERS + 1,)), dma((ITERS,)), dma((ITERS,)), dma, dma,
            dma((2, 2, 4)), dma((2, 2, 4)), dma((2,)), dma((2,)),
        ],
        compiler_params=pltpu.CompilerParams(
            collective_id=0, has_side_effects=True, vmem_limit_bytes=40 * 2**20
        ),
        name="coupling",
    )(noise, data)
    return (targets, noise_pot[0], data_pot[0])


def solution(mesh):
    placed = (P("row", "col"), P("col", "row"))
    return jax.shard_map(
        per_device,
        mesh=mesh,
        in_specs=placed,
        out_specs=(P(("row", "col"), None), P("row"), P("col")),
        check_vma=False,
    )
```

time: 874 us -> 133 us (0.15)
  the two profiles are of different devices: /device:TPU:2 before, /device:TPU:8 now
where the time goes in v2:
time: 133 us
  Pallas kernels  128 us (96%)
  local copies, waits for them, and re-layouts  3.67 us (3%)
    pallas_call x1, Pallas kernels, per_device(): pl.pallas_call(kernel, out_shape=(jax.ShapeDtypeStruct((8, LATENT), BF16)...  128 us
    unnamed x7, local copies, waits for them, and re-layouts  3.67 us

profile of v2, /device:TPU:8, one launch (start us, length us, event | category | flops | bytes accessed | tf_op | source)
XLA Modules:
  0.0 132.6 jit_solution(14264097012185667075)
XLA Ops:
  0.6 0.0 copy-start
  0.6 0.9 copy-done
  1.6 0.0 copy-start.1
  1.6 0.9 copy-done.1
  2.5 128.3 %coupling.1 = (bf16[8,16384]{1,0:T(8,128)(2,1)S(1)}, f32[1,128]{1,0:T(1,128)S(1)}, f32[1,256]{1,0:T(1,128)S(1)}) custom-call(bf16[128,1024]{1,0:T(8,128)(2,1)S(1)} %copy-done, bf16[256,512]{1,0:T(8,128)(2,1)S(1)} %copy-done.1), custom_call_target="tpu_custom_call" | custom-call | tf_op jit(solution)/shard_map/coupling/pallas_call | solution.py:335
  130.8 0.7 copy.8
  131.5 0.5 copy.9
  132.1 0.6 copy.10
Async XLA Ops:
  0.6 1.0 copy-start
  1.6 0.9 copy-start.1

commit v3 on v2

v3 whole, which is shorter than its diff:
```python
import math

import jax
import jax.numpy as jnp
from jax import lax
from jax.experimental import pallas as pl
from jax.experimental.pallas import tpu as pltpu
from jax.sharding import PartitionSpec as P

LATENT = 16384
ITERS = 3
X, Y, Z = 4, 8, 8
N_ROW, N_COL = X * Y, 2 * Z
ROWS, COLS = 128, 256
LOG_COUNT = math.log(4096)
EPSILON = 0.64 / math.sqrt(LATENT)
BLOCK = 512
CHUNKS = 4
CHUNK = 256 // CHUNKS
MESH = pl.DeviceIdType.MESH
F32, BF16 = jnp.float32, jnp.bfloat16


def flip(line, copies):
    return jnp.transpose(jnp.broadcast_to(line, (copies, line.shape[1])))


def squares(block):
    block = jnp.square(block.astype(F32))
    return sum(block[:, i : i + 128] for i in range(0, block.shape[1], 128))


def hops(way, half):
    return 4 if way == half else 3


def legs(way, chunk):
    return hops(way, chunk // (CHUNKS // 2))


def kernel(
    noise_hbm, data_hbm, out_ref, noise_pot_ref, data_pot_ref,
    noise_ref, in_sem, nb, dd, part, part_in, square_sum, norm_slots, score, score_t, f_slots, g_slots,
    w_send, w_all, scales, po, rs_in, rs_out, fin_send, fin_in,
    own_send, own_recv, ring_send, ring_recv, pair_send, pair_recv, dpair_send, dpair_recv,
    part_s, part_r, norm_s, norm_r, f_send, f_recv, g_send, g_recv, w_s, w_r, sc_s, sc_r,
    rs_s, rs_r, fin_s, fin_r,
):
    row, col = lax.axis_index("row"), lax.axis_index("col")
    y, x = row // X, lax.rem(row, X)
    z, c = col // 2, lax.rem(col, 2)
    other = 1 - c

    def at(y_, x_, z_, c_):
        return (y_ * X + x_, z_ * 2 + c_)

    def wrap(i, n):
        return lax.rem(i + n, n)

    def send(src, dst, send_sem, recv_sem, device):
        return pltpu.make_async_remote_copy(
            src_ref=src, dst_ref=dst, send_sem=send_sem, recv_sem=recv_sem,
            device_id=device, device_id_type=MESH,
        )

    def take(ref, sem):
        pltpu.make_async_copy(ref, ref, sem).wait()

    drains = []
    barrier = pltpu.get_barrier_semaphore()
    near = [at(wrap(y + 1, Y), x, z, c), at(wrap(y - 1, Y), x, z, c)]
    near += [at(y, x, wrap(z + 1, Z), c), at(y, x, wrap(z - 1, Z), c), at(y, x, z, other)]
    for k in range(1, X):
        near += [at(y, wrap(x + k, X), z, c), at(y, wrap(x + k, X), z, other)]
    for device in near:
        pl.semaphore_signal(barrier, inc=1, device_id=device, device_id_type=MESH)
    data_ref = dd.at[c, y]
    noise_in = pltpu.make_async_copy(noise_hbm, noise_ref, in_sem.at[0])
    data_in = pltpu.make_async_copy(data_hbm, data_ref, in_sem.at[1])
    noise_in.start()
    data_in.start()
    part[...] = jnp.zeros_like(part)
    noise_in.wait()
    data_in.wait()
    pl.semaphore_wait(barrier, len(near))

    mine = x // 2 == c
    first = jnp.where(mine, lax.rem(x, 2), 1 - lax.rem(x, 2))

    def noise_chunk(block, core, chunk):
        half, rest = chunk // (CHUNKS // 2), chunk % (CHUNKS // 2)
        begin = core * 256 + jnp.where(first == half, 0, 1) * 128 + rest * CHUNK
        return nb.at[block, pl.ds(pl.multiple_of(begin, CHUNK), CHUNK)]

    def ring(kind, way, chunk, step):
        place = (y, z)[kind]
        sign = 1 - 2 * way
        block = wrap(place - sign * (step - 1), 8)
        target = wrap(place + sign, 8)
        if kind == 0:
            ref = dd.at[c, block, pl.ds(chunk * CHUNK, CHUNK)]
            device = at(target, x, z, c)
        else:
            ref = noise_chunk(block, c, chunk)
            device = at(y, x, target, c)
        index = (kind, way, chunk, step - 1)
        return send(ref, ref, ring_send.at[index], ring_recv.at[index], device)

    n1_device = [at(y, 2 * c + h, z, x // 2) for h in range(2)]
    n1_self = [jnp.logical_and(mine, lax.rem(x, 2) == h) for h in range(2)]
    n1 = []
    for rest in range(CHUNKS // 2):
        for h in range(2):
            src = noise_ref.at[pl.ds(rest * CHUNK, CHUNK), pl.ds(h * BLOCK, BLOCK)]
            dst = nb.at[z, pl.ds(pl.multiple_of(x * ROWS + rest * CHUNK, CHUNK), CHUNK)]
            sem = own_recv.at[lax.rem(x, 2), rest]
            far = send(src, dst, own_send.at[h, rest], sem, n1_device[h])
            near_copy = pltpu.make_async_copy(src, dst, sem)
            n1.append((h, far))

            @pl.when(n1_self[h])
            def _():
                near_copy.start()

            @pl.when(jnp.logical_not(n1_self[h]))
            def _():
                far.start()

    for chunk in range(CHUNKS):
        for way in range(2):
            ring(0, way, chunk, 1).start()

    def pair(way, chunk, step, block):
        index = (way, chunk, step)
        ref = noise_chunk(block, c, chunk)
        return send(ref, ref, pair_send.at[index], pair_recv.at[index], at(y, x, z, other))

    pairs = []
    for chunk in range(CHUNKS):
        half, rest = chunk // (CHUNKS // 2), chunk % (CHUNKS // 2)
        parity = jnp.where(first == half, 0, 1)
        take(noise_chunk(z, c, chunk), own_recv.at[parity, rest])
        for way in range(2):
            ring(1, way, chunk, 1).start()
        pairs.append(pair(0, chunk, 0, z))
        pairs[-1].start()

    square_sum[...] = squares(data_ref[...])
    last_data, last_noise = wrap(y + 4, Y), wrap(z + 4, Z)

    def product(a, b):
        return lax.dot_general(a, b, (((1,), (1,)), ((), ())), preferred_element_type=F32)

    for step in range(1, 5):
        for chunk in range(CHUNKS):
            for kind in range(2):
                for way in range(2):
                    if step > legs(way, chunk):
                        continue
                    ring(kind, way, chunk, step).wait_recv()
                    if step < legs(way, chunk):
                        ring(kind, way, chunk, step + 1).start()
                    if kind == 1:
                        block = wrap(z - (1 - 2 * way) * step, Z)
                        pairs.append(pair(way, chunk, step, block))
                        pairs[-1].start()
        if step < 4:
            for block in (wrap(y - step, Y), wrap(y + step, Y)):
                square_sum[...] += squares(dd[c, block])
        if step == 3:
            for copy in pairs:
                copy.wait_recv()
            early = len(pairs)

            @pl.loop(0, Y)
            def _(k):
                @pl.when(jnp.logical_and(k != last_data, k != last_noise))
                def _():
                    part[...] += product(nb[k], dd[c, k])
    for copy in pairs[early:]:
        copy.wait_recv()

    def drain_rings():
        for h, far in n1:
            @pl.when(jnp.logical_not(n1_self[h]))
            def _():
                far.wait_send()
        for kind in range(2):
            for chunk in range(CHUNKS):
                for way in range(2):
                    for step in range(1, legs(way, chunk) + 1):
                        ring(kind, way, chunk, step).wait_send()
        for copy in pairs:
            copy.wait_send()
    drains.append(drain_rings)
    part_copies = []
    for k in (2, 1, 3, 0):
        target = wrap(x + k, X)
        rows = pl.ds(pl.multiple_of(target * ROWS, ROWS), ROWS)
        part[rows, :] += product(nb[last_data, rows, :], dd[c, last_data])

        @pl.when(last_data != last_noise)
        def _():
            part[rows, :] += product(nb[last_noise, rows, :], dd[c, last_noise])

        if k:
            copy = send(
                part.at[rows], part_in.at[k - 1], part_s.at[k - 1], part_r.at[k - 1],
                at(y, target, z, c),
            )
            copy.start()
            part_copies.append(copy)
    square_sum[...] += squares(dd[c, wrap(y + 4, Y)])
    norm_slots[x] = jnp.sum(jnp.transpose(square_sum[...]), axis=0, keepdims=True)
    for k in range(1, X):
        send(
            norm_slots.at[x], norm_slots.at[x], norm_s, norm_r, at(y, wrap(x + k, X), z, c)
        ).start()
    fold = squares(noise_ref[...])
    noise_squares = jnp.sum(jnp.transpose(fold), axis=0, keepdims=True)
    for copy in part_copies:
        copy.wait_recv()
    total = part[pl.ds(pl.multiple_of(x * ROWS, ROWS), ROWS), :]
    total = total + part_in[0] + part_in[1] + part_in[2]
    score[...] = total * (2.0 / LATENT / EPSILON)
    score_t[...] = jnp.transpose(score[...])
    take(norm_slots.at[pl.ds(0, X - 1)], norm_r)
    data_norm = (norm_slots[0] + norm_slots[1] + norm_slots[2] + norm_slots[3]) / LATENT

    def drain_parts():
        for copy in part_copies:
            copy.wait_send()
        take(norm_slots.at[pl.ds(0, X - 1)], norm_s)
    drains.append(drain_parts)
    dpair = send(dd.at[c], dd.at[c], dpair_send, dpair_recv, at(y, x, z, other))
    dpair.start()

    def far_first(i, n):
        return n // 2 + (1 - 2 * lax.rem(i, 2)) * ((i + 1) // 2)

    def along_col(k):
        i = (k - 1) // 2
        return at(y, x, wrap(z + far_first(i, Z), Z), wrap(c + lax.rem(k, 2), 2))

    def along_row(k):
        i, j = (k - 1) // X, lax.rem(k - 1, X)
        return at(wrap(y + far_first(i, Y), Y), wrap(x + far_first(j, X), X), z, c)

    def post(scores, slots, step, me, count, target, send_sem, recv_sem):
        peak = jnp.max(scores, axis=0, keepdims=True)
        slots[step, me, 0:1, :] = peak
        slots[step, me, 1:2, :] = jnp.sum(jnp.exp(scores - peak), axis=0, keepdims=True)

        @pl.loop(1, count)
        def _(k):
            ref = slots.at[step, me]
            send(ref, ref, send_sem.at[step], recv_sem.at[step], target(k)).start()

        return peak

    def merge(slots, step, count, recv_sem):
        take(slots.at[step, pl.ds(0, count - 1)], recv_sem.at[step])
        peaks, sums = slots[step, :, 0, :], slots[step, :, 1, :]
        peak = jnp.max(peaks, axis=0, keepdims=True)
        total = jnp.sum(sums * jnp.exp(peaks - peak), axis=0, keepdims=True)
        return -(LOG_COUNT + peak + jnp.log(total))

    def wide(u):
        tile = flip(u, 128)
        return jnp.concatenate([tile] * (COLS // 128), axis=1)

    def post_noise(step, v):
        f_slots[step, col, 2:3, :] = noise_squares
        scores = score_t[...] + flip(v, ROWS)
        return post(scores, f_slots, step, col, N_COL, along_col, f_send, f_recv)

    def post_data(step, u):
        scores = score[...] + wide(u)
        return post(scores, g_slots, step, row, N_ROW, along_row, g_send, g_recv)

    v = -data_norm / EPSILON
    for step in range(ITERS):
        post_noise(step, v)
        u = merge(f_slots, step, N_COL, f_recv)
        post_data(step, u)
        v = merge(g_slots, step, N_ROW, g_recv)
    peak = post_noise(ITERS, v)

    def to_group(src, dst, send_sem, recv_sem):
        for k in (2, 1, 3, 0):
            for flipped in (1, 0):
                if k == 0 and flipped == 0:
                    continue
                core = wrap(c + flipped, 2)
                send(src(core), dst, send_sem, recv_sem, at(y, wrap(x + k, X), z, core)).start()

    member = c * X + x
    raw = jnp.exp(score[...] + v - wide(peak)).reshape(Z, 2, 8, COLS)
    for core in range(2):
        w_send[core] = raw[:, core].reshape(Z * 8, COLS).astype(BF16)
    to_group(lambda core: w_send.at[core], w_all.at[member], w_s, w_r)
    w_all[member] = w_send[c]
    u = merge(f_slots, ITERS, N_COL, f_recv)
    scales[member] = jnp.exp(u + peak + LOG_COUNT)
    to_group(lambda core: scales.at[member], scales.at[member], sc_s, sc_r)
    noise_norm = jnp.sum(f_slots[0, :, 2, :], axis=0, keepdims=True) / LATENT
    noise_pot_ref[...] = EPSILON * u + noise_norm
    data_pot_ref[...] = EPSILON * v + data_norm
    dpair.wait_recv()

    def drain_sink():
        for step in range(ITERS + 1):
            take(f_slots.at[step, pl.ds(0, N_COL - 1)], f_send.at[step])
        for step in range(ITERS):
            take(g_slots.at[step, pl.ds(0, N_ROW - 1)], g_send.at[step])
    drains.append(drain_sink)
    drains.append(dpair.wait_send)
    take(w_all.at[pl.ds(0, 2 * X - 1)], w_r)
    take(scales.at[pl.ds(0, 2 * X - 1)], sc_r)
    factors = jnp.transpose(scales[:, 0, :]).reshape(Z, 2, 8, 2 * X)
    factors = jnp.where(c == 0, factors[:, 0], factors[:, 1]).reshape(Z * 8, 2 * X)
    for k in range(2 * X):
        w_all[k] = (w_all[k].astype(F32) * factors[:, k : k + 1]).astype(BF16)
    drains.append(lambda: take(w_all.at[pl.ds(0, 2 * X - 1)], w_s))
    drains.append(lambda: take(scales.at[pl.ds(0, 2 * X - 1)], sc_s))
    def rs(way, half, step):
        sign = 1 - 2 * way
        index = (way, half, step - 1)
        if step == 1:
            src = po.at[half, wrap(z + sign * hops(way, half), Z)]
        else:
            src = rs_out.at[way, half, step - 2]
        return send(
            src, rs_in.at[index], rs_s.at[index], rs_r.at[index], at(y, x, wrap(z + sign, Z), c)
        )

    for half in range(2):
        @pl.loop(0, Y // 2)
        def _(j):
            block = half * (Y // 2) + j
            sums = jnp.dot(
                w_all[0:X].reshape(256, COLS), dd[0, block], preferred_element_type=F32
            ) + jnp.dot(w_all[X:].reshape(256, COLS), dd[1, block], preferred_element_type=F32)
            sums = sums.reshape(X, Z, 8, BLOCK)
            columns = pl.ds(pl.multiple_of(j * BLOCK, BLOCK), BLOCK)
            for k in range(Z):
                po[half, k, :, columns] = sums[:, k].reshape(X * 8, BLOCK).astype(BF16)

        for way in range(2):
            rs(way, half, 1).start()

    def finish(half):
        sums = po[half, z].astype(F32)
        for way in range(2):
            sums = sums + rs_in[way, half, hops(way, half) - 1].astype(F32)
        for k in range(X):
            lines = sums[k * 8 : k * 8 + 8]
            lines = jnp.concatenate([lines[:, :1024], lines[:, 1024:]], axis=0)
            fin_send[half, k] = lines.astype(BF16)
        for k in (2, 1, 3):
            target = wrap(x + k, X)
            send(
                fin_send.at[half, target], fin_in.at[half, x], fin_s.at[half], fin_r.at[half],
                at(y, target, z, c),
            ).start()
        fin_in[half, x] = fin_send[half, x]

    for step in range(1, 5):
        for half in range(2):
            for way in range(2):
                if step > hops(way, half):
                    continue
                rs(way, half, step).wait_recv()
                if step < hops(way, half):
                    target = wrap(z + (1 - 2 * way) * (hops(way, half) - step), Z)
                    rs_out[way, half, step - 1] = (
                        rs_in[way, half, step - 1].astype(F32) + po[half, target].astype(F32)
                    ).astype(BF16)
                    rs(way, half, step + 1).start()
            if step == 4:
                finish(half)

    def drain_rs():
        for half in range(2):
            for way in range(2):
                for step in range(1, hops(way, half) + 1):
                    rs(way, half, step).wait_send()
    drains.append(drain_rs)
    for half in range(2):
        take(fin_in.at[half, pl.ds(0, X - 1)], fin_r.at[half])
        for k in range(X):
            lines = fin_in[half, k].astype(F32)
            for quarter in range(2):
                for part_block in range(2):
                    block = half * 4 + quarter * 2 + part_block
                    begin = (block * X + k) * BLOCK
                    out_ref[:, begin : begin + BLOCK] = lines[
                        quarter * 8 : quarter * 8 + 8, part_block * BLOCK : (part_block + 1) * BLOCK
                    ].astype(BF16)

    def drain_fin():
        for half in range(2):
            take(fin_in.at[half, pl.ds(0, X - 1)], fin_s.at[half])
    drains.append(drain_fin)
    for d in drains:
        d()


def per_device(noise, data):
    vmem = pl.BlockSpec(memory_space=pltpu.VMEM)
    dma = pltpu.SemaphoreType.DMA
    targets, noise_pot, data_pot = pl.pallas_call(
        kernel,
        out_shape=(
            jax.ShapeDtypeStruct((8, LATENT), BF16),
            jax.ShapeDtypeStruct((1, ROWS), F32),
            jax.ShapeDtypeStruct((1, COLS), F32),
        ),
        in_specs=[pl.BlockSpec(memory_space=pltpu.HBM)] * 2,
        out_specs=(vmem, vmem, vmem),
        scratch_shapes=[
            pltpu.VMEM((ROWS, 1024), BF16), dma((2,)),
            pltpu.VMEM((Z, X * ROWS, BLOCK), BF16),
            pltpu.VMEM((2, Y, COLS, BLOCK), BF16),
            pltpu.VMEM((X * ROWS, COLS), F32),
            pltpu.VMEM((X - 1, ROWS, COLS), F32),
            pltpu.VMEM((COLS, 128), F32),
            pltpu.VMEM((X, 1, COLS), F32),
            pltpu.VMEM((ROWS, COLS), F32),
            pltpu.VMEM((COLS, ROWS), F32),
            pltpu.VMEM((ITERS + 1, N_COL, 3, ROWS), F32),
            pltpu.VMEM((ITERS, N_ROW, 2, COLS), F32),
            pltpu.VMEM((2, Z * 8, COLS), BF16),
            pltpu.VMEM((2 * X, Z * 8, COLS), BF16),
            pltpu.VMEM((2 * X, 1, ROWS), F32),
            pltpu.VMEM((2, Z, X * 8, 2048), BF16),
            pltpu.VMEM((2, 2, 4, X * 8, 2048), BF16),
            pltpu.VMEM((2, 2, 3, X * 8, 2048), BF16),
            pltpu.VMEM((2, X, 16, 1024), BF16),
            pltpu.VMEM((2, X, 16, 1024), BF16),
            dma((2, CHUNKS // 2)), dma((2, CHUNKS // 2)),
            dma((2, 2, CHUNKS, 4)), dma((2, 2, CHUNKS, 4)),
            dma((2, CHUNKS, 5)), dma((2, CHUNKS, 5)), dma, dma,
            dma((3,)), dma((3,)), dma, dma,
            dma((ITERS + 1,)), dma((ITERS + 1,)), dma((ITERS,)), dma((ITERS,)), dma, dma, dma, dma,
            dma((2, 2, 4)), dma((2, 2, 4)), dma((2,)), dma((2,)),
        ],
        compiler_params=pltpu.CompilerParams(
            collective_id=0, has_side_effects=True, vmem_limit_bytes=60 * 2**20
        ),
        name="coupling",
    )(noise, data)
    return (targets, noise_pot[0], data_pot[0])


def solution(mesh):
    placed = (P("row", "col"), P("col", "row"))
    return jax.shard_map(
        per_device,
        mesh=mesh,
        in_specs=placed,
        out_specs=(P(("row", "col"), None), P("row"), P("col")),
        check_vma=False,
    )
```

time: 133 us -> 126 us (0.947)
  Pallas kernels: 128 us -> 122 us
    pallas_call x1, Pallas kernels: 128 us -> 122 us  [per_device(): pl.pallas_call(kernel, out_shape=(jax.ShapeDtypeStruct((8, LATENT), BF16)...]
where the time goes in v3:
time: 126 us
  Pallas kernels  122 us (97%)
  local copies, waits for them, and re-layouts  2.91 us (2%)
    pallas_call x1, Pallas kernels, per_device(): pl.pallas_call(kernel, out_shape=(jax.ShapeDtypeStruct((8, LATENT), BF16)...  122 us
    unnamed x7, local copies, waits for them, and re-layouts  2.91 us

profile of v3, /device:TPU:8, one launch (start us, length us, event | category | flops | bytes accessed | tf_op | source)
XLA Modules:
  0.0 125.7 jit_solution(5630070888832364318)
XLA Ops:
  0.6 122.1 %coupling.1 = (bf16[8,16384]{1,0:T(8,128)(2,1)}, f32[1,128]{1,0:T(1,128)}, f32[1,256]{1,0:T(1,128)}) custom-call(bf16[128,1024]{1,0:T(8,128)(2,1)} %noise_hbm.1, bf16[256,512]{1,0:T(8,128)(2,1)} %data_hbm.1), custom_call_target="tpu_custom_call" | custom-call | tf_op jit(solution)/shard_map/coupling/pallas_call | solution.py:412
  122.8 0.0 copy-start.1
  122.8 1.7 %copy.8 = bf16[8,16384]{1,0:T(8,128)(2,1)} copy(bf16[8,16384]{1,0:T(8,128)(2,1)} %get-tuple-element.12) | data formatting | bytes 524288
  124.4 0.0 copy-done.1
  124.4 0.0 copy-start
  124.4 0.5 copy.9
  124.9 0.2 copy-done
  125.1 0.6 copy.10
Async XLA Ops:
  122.8 1.7 %copy-start.1 = (f32[1,128]{1,0:T(1,128)S(1)}, f32[1,128]{1,0:T(1,128)}, u32[]{:S(2)}) copy-start(f32[1,128]{1,0:T(1,128)} %get-tuple-element.7) | copy-start | bytes 1540
  124.4 0.7 copy-start

commit v4 on v3

--- a/solution.py
+++ b/solution.py
@@ -1,3 +1,4 @@
+import functools
 import math
 
 import jax
@@ -41,9 +42,9 @@
 def kernel(
     noise_hbm, data_hbm, out_ref, noise_pot_ref, data_pot_ref,
     noise_ref, in_sem, nb, dd, part, part_in, square_sum, norm_slots, score, score_t, f_slots, g_slots,
-    w_send, w_all, scales, po, rs_in, rs_out, fin_send, fin_in,
+    w_send, w_all, h_slots, po, rs_in, rs_out, fin_send, fin_in,
     own_send, own_recv, ring_send, ring_recv, pair_send, pair_recv, dpair_send, dpair_recv,
-    part_s, part_r, norm_s, norm_r, f_send, f_recv, g_send, g_recv, w_s, w_r, sc_s, sc_r,
+    part_s, part_r, norm_s, norm_r, f_send, f_recv, g_send, g_recv, w_s, w_r, h_send, h_recv,
     rs_s, rs_r, fin_s, fin_r,
 ):
     row, col = lax.axis_index("row"), lax.axis_index("col")
@@ -67,6 +68,11 @@
         pltpu.make_async_copy(ref, ref, sem).wait()
 
     drains = []
+
+    def flush():
+        while drains:
+            drains.pop(0)()
+
     barrier = pltpu.get_barrier_semaphore()
     near = [at(wrap(y + 1, Y), x, z, c), at(wrap(y - 1, Y), x, z, c)]
     near += [at(y, x, wrap(z + 1, Z), c), at(y, x, wrap(z - 1, Z), c), at(y, x, z, other)]
@@ -104,7 +110,7 @@
             ref = noise_chunk(block, c, chunk)
             device = at(y, x, target, c)
         index = (kind, way, chunk, step - 1)
-        return send(ref, ref, ring_send.at[index], ring_recv.at[index], device)
+        return send(ref, ref, ring_send.at[kind], ring_recv.at[index], device)
 
     n1_device = [at(y, 2 * c + h, z, x // 2) for h in range(2)]
     n1_self = [jnp.logical_and(mine, lax.rem(x, 2) == h) for h in range(2)]
@@ -133,7 +139,7 @@
     def pair(way, chunk, step, block):
         index = (way, chunk, step)
         ref = noise_chunk(block, c, chunk)
-        return send(ref, ref, pair_send.at[index], pair_recv.at[index], at(y, x, z, other))
+        return send(ref, ref, pair_send, pair_recv.at[index], at(y, x, z, other))
 
     pairs = []
     for chunk in range(CHUNKS):
@@ -185,13 +191,9 @@
             @pl.when(jnp.logical_not(n1_self[h]))
             def _():
                 far.wait_send()
-        for kind in range(2):
-            for chunk in range(CHUNKS):
-                for way in range(2):
-                    for step in range(1, legs(way, chunk) + 1):
-                        ring(kind, way, chunk, step).wait_send()
-        for copy in pairs:
-            copy.wait_send()
+        take(dd.at[c, pl.ds(0, Y - 1)], ring_send.at[0])
+        take(nb.at[pl.ds(0, Z - 1), pl.ds(0, 256)], ring_send.at[1])
+        take(nb.at[:, pl.ds(0, 256)], pair_send)
     drains.append(drain_rings)
     part_copies = []
     for k in (2, 1, 3, 0):
@@ -233,7 +235,6 @@
         take(norm_slots.at[pl.ds(0, X - 1)], norm_s)
     drains.append(drain_parts)
     dpair = send(dd.at[c], dd.at[c], dpair_send, dpair_recv, at(y, x, z, other))
-    dpair.start()
 
     def far_first(i, n):
         return n // 2 + (1 - 2 * lax.rem(i, 2)) * ((i + 1) // 2)
@@ -241,6 +242,11 @@
     def along_col(k):
         i = (k - 1) // 2
         return at(y, x, wrap(z + far_first(i, Z), Z), wrap(c + lax.rem(k, 2), 2))
+
+    def along_both(k):
+        i, j = (k - 1) // (2 * X), lax.rem((k - 1) // 2, X)
+        z_, x_ = wrap(z + far_first(i, Z), Z), wrap(x + far_first(j, X), X)
+        return at(y, x_, z_, wrap(c + lax.rem(k, 2), 2))
 
     def along_row(k):
         i, j = (k - 1) // X, lax.rem(k - 1, X)
@@ -260,7 +266,13 @@
 
     def merge(slots, step, count, recv_sem):
         take(slots.at[step, pl.ds(0, count - 1)], recv_sem.at[step])
-        peaks, sums = slots[step, :, 0, :], slots[step, :, 1, :]
+        return combine(slots[step])
+
+    def drain(slots, step, count, send_sem):
+        take(slots.at[step, pl.ds(0, count - 1)], send_sem.at[step])
+
+    def combine(slots):
+        peaks, sums = slots[:, 0, :], slots[:, 1, :]
         peak = jnp.max(peaks, axis=0, keepdims=True)
         total = jnp.sum(sums * jnp.exp(peaks - peak), axis=0, keepdims=True)
         return -(LOG_COUNT + peak + jnp.log(total))
@@ -281,10 +293,18 @@
     v = -data_norm / EPSILON
     for step in range(ITERS):
         post_noise(step, v)
+        flush()
+        drains.append(functools.partial(drain, f_slots, step, N_COL, f_send))
         u = merge(f_slots, step, N_COL, f_recv)
         post_data(step, u)
+        if step == 0:
+            dpair.start()
+        flush()
+        drains.append(functools.partial(drain, g_slots, step, N_ROW, g_send))
         v = merge(g_slots, step, N_ROW, g_recv)
-    peak = post_noise(ITERS, v)
+    scores = score_t[...] + flip(v, ROWS)
+    peak = post(scores, h_slots, 0, x * N_COL + col, X * N_COL, along_both, h_send, h_recv)
+    flush()
 
     def to_group(src, dst, send_sem, recv_sem):
         for k in (2, 1, 3, 0):
@@ -300,29 +320,29 @@
         w_send[core] = raw[:, core].reshape(Z * 8, COLS).astype(BF16)
     to_group(lambda core: w_send.at[core], w_all.at[member], w_s, w_r)
     w_all[member] = w_send[c]
-    u = merge(f_slots, ITERS, N_COL, f_recv)
-    scales[member] = jnp.exp(u + peak + LOG_COUNT)
-    to_group(lambda core: scales.at[member], scales.at[member], sc_s, sc_r)
+    drains.append(lambda: take(h_slots.at[0, pl.ds(0, X * N_COL - 1)], h_send.at[0]))
+    take(h_slots.at[0, pl.ds(0, X * N_COL - 1)], h_recv.at[0])
+    us, factors = [], [None] * (2 * X)
+    for k in range(X):
+        us.append(combine(h_slots[0, pl.ds(k * N_COL, N_COL)]))
+        for core in range(2):
+            source = h_slots[0, k * N_COL + z * 2 + core]
+            factors[core * X + k] = jnp.exp(us[k] + source[0:1, :] + LOG_COUNT)
+    u = us[0]
+    for k in range(1, X):
+        u = jnp.where(x == k, us[k], u)
     noise_norm = jnp.sum(f_slots[0, :, 2, :], axis=0, keepdims=True) / LATENT
     noise_pot_ref[...] = EPSILON * u + noise_norm
     data_pot_ref[...] = EPSILON * v + data_norm
     dpair.wait_recv()
 
-    def drain_sink():
-        for step in range(ITERS + 1):
-            take(f_slots.at[step, pl.ds(0, N_COL - 1)], f_send.at[step])
-        for step in range(ITERS):
-            take(g_slots.at[step, pl.ds(0, N_ROW - 1)], g_send.at[step])
-    drains.append(drain_sink)
     drains.append(dpair.wait_send)
     take(w_all.at[pl.ds(0, 2 * X - 1)], w_r)
-    take(scales.at[pl.ds(0, 2 * X - 1)], sc_r)
-    factors = jnp.transpose(scales[:, 0, :]).reshape(Z, 2, 8, 2 * X)
+    factors = jnp.transpose(jnp.concatenate(factors, axis=0)).reshape(Z, 2, 8, 2 * X)
     factors = jnp.where(c == 0, factors[:, 0], factors[:, 1]).reshape(Z * 8, 2 * X)
     for k in range(2 * X):
         w_all[k] = (w_all[k].astype(F32) * factors[:, k : k + 1]).astype(BF16)
     drains.append(lambda: take(w_all.at[pl.ds(0, 2 * X - 1)], w_s))
-    drains.append(lambda: take(scales.at[pl.ds(0, 2 * X - 1)], sc_s))
     def rs(way, half, step):
         sign = 1 - 2 * way
         index = (way, half, step - 1)
@@ -365,6 +385,7 @@
             ).start()
         fin_in[half, x] = fin_send[half, x]
 
+    flush()
     for step in range(1, 5):
         for half in range(2):
             for way in range(2):
@@ -385,7 +406,7 @@
             for way in range(2):
                 for step in range(1, hops(way, half) + 1):
                     rs(way, half, step).wait_send()
-    drains.append(drain_rs)
+    drain_rs()
     for half in range(2):
         take(fin_in.at[half, pl.ds(0, X - 1)], fin_r.at[half])
         for k in range(X):
@@ -402,8 +423,7 @@
         for half in range(2):
             take(fin_in.at[half, pl.ds(0, X - 1)], fin_s.at[half])
     drains.append(drain_fin)
-    for d in drains:
-        d()
+    flush()
 
 
 def per_device(noise, data):
@@ -428,21 +448,21 @@
             pltpu.VMEM((X, 1, COLS), F32),
             pltpu.VMEM((ROWS, COLS), F32),
             pltpu.VMEM((COLS, ROWS), F32),
-            pltpu.VMEM((ITERS + 1, N_COL, 3, ROWS), F32),
+            pltpu.VMEM((ITERS, N_COL, 3, ROWS), F32),
             pltpu.VMEM((ITERS, N_ROW, 2, COLS), F32),
             pltpu.VMEM((2, Z * 8, COLS), BF16),
             pltpu.VMEM((2 * X, Z * 8, COLS), BF16),
-            pltpu.VMEM((2 * X, 1, ROWS), F32),
+            pltpu.VMEM((1, X * N_COL, 2, ROWS), F32),
             pltpu.VMEM((2, Z, X * 8, 2048), BF16),
             pltpu.VMEM((2, 2, 4, X * 8, 2048), BF16),
             pltpu.VMEM((2, 2, 3, X * 8, 2048), BF16),
             pltpu.VMEM((2, X, 16, 1024), BF16),
             pltpu.VMEM((2, X, 16, 1024), BF16),
             dma((2, CHUNKS // 2)), dma((2, CHUNKS // 2)),
-            dma((2, 2, CHUNKS, 4)), dma((2, 2, CHUNKS, 4)),
-            dma((2, CHUNKS, 5)), dma((2, CHUNKS, 5)), dma, dma,
+            dma((2,)), dma((2, 2, CHUNKS, 4)),
+            dma, dma((2, CHUNKS, 5)), dma, dma,
             dma((3,)), dma((3,)), dma, dma,
-            dma((ITERS + 1,)), dma((ITERS + 1,)), dma((ITERS,)), dma((ITERS,)), dma, dma, dma, dma,
+            dma((ITERS,)), dma((ITERS,)), dma((ITERS,)), dma((ITERS,)), dma, dma, dma((1,)), dma((1,)),
             dma((2, 2, 4)), dma((2, 2, 4)), dma((2,)), dma((2,)),
         ],
         compiler_params=pltpu.CompilerParams(

time: 126 us -> 124 us (0.984)
  Pallas kernels: 122 us -> 120 us
    pallas_call x1, Pallas kernels: 122 us -> 120 us  [per_device(): pl.pallas_call(kernel, out_shape=(jax.ShapeDtypeStruct((8, LATENT), BF16)...]
where the time goes in v4:
time: 124 us; the launch traced here: 123 us
  Pallas kernels  120 us (97%)
  local copies, waits for them, and re-layouts  2.91 us (2%)
    pallas_call x1, Pallas kernels, per_device(): pl.pallas_call(kernel, out_shape=(jax.ShapeDtypeStruct((8, LATENT), BF16)...  120 us
    unnamed x7, local copies, waits for them, and re-layouts  2.91 us

profile of v4, /device:TPU:8, one launch (start us, length us, event | category | flops | bytes accessed | tf_op | source)
XLA Modules:
  0.0 123.5 jit_solution(1212622460418832360)
XLA Ops:
  0.6 119.9 %coupling.1 = (bf16[8,16384]{1,0:T(8,128)(2,1)}, f32[1,128]{1,0:T(1,128)}, f32[1,256]{1,0:T(1,128)}) custom-call(bf16[128,1024]{1,0:T(8,128)(2,1)} %noise_hbm.1, bf16[256,512]{1,0:T(8,128)(2,1)} %data_hbm.1), custom_call_target="tpu_custom_call" | custom-call | tf_op jit(solution)/shard_map/coupling/pallas_call | solution.py:432
  120.6 0.0 copy-start.1
  120.6 1.7 %copy.8 = bf16[8,16384]{1,0:T(8,128)(2,1)} copy(bf16[8,16384]{1,0:T(8,128)(2,1)} %get-tuple-element.12) | data formatting | bytes 524288
  122.2 0.0 copy-done.1
  122.3 0.0 copy-start
  122.3 0.5 copy.9
  122.8 0.2 copy-done
  122.9 0.6 copy.10
Async XLA Ops:
  120.6 1.7 %copy-start.1 = (f32[1,128]{1,0:T(1,128)S(1)}, f32[1,128]{1,0:T(1,128)}, u32[]{:S(2)}) copy-start(f32[1,128]{1,0:T(1,128)} %get-tuple-element.7) | copy-start | bytes 1540
  122.3 0.7 copy-start

commit v5 on v4

--- a/solution.py
+++ b/solution.py
@@ -18,6 +18,8 @@
 BLOCK = 512
 CHUNKS = 4
 CHUNK = 256 // CHUNKS
+PIECES = 4
+PIECE = Y * BLOCK // PIECES
 MESH = pl.DeviceIdType.MESH
 F32, BF16 = jnp.float32, jnp.bfloat16
 
@@ -37,6 +39,10 @@
 
 def legs(way, chunk):
     return hops(way, chunk // (CHUNKS // 2))
+
+
+def turns(way, piece):
+    return hops(way, piece // (PIECES // 2))
 
 
 def kernel(
@@ -343,85 +349,84 @@
     for k in range(2 * X):
         w_all[k] = (w_all[k].astype(F32) * factors[:, k : k + 1]).astype(BF16)
     drains.append(lambda: take(w_all.at[pl.ds(0, 2 * X - 1)], w_s))
-    def rs(way, half, step):
+    def rs(way, piece, step):
         sign = 1 - 2 * way
-        index = (way, half, step - 1)
+        index = (way, piece, step - 1)
         if step == 1:
-            src = po.at[half, wrap(z + sign * hops(way, half), Z)]
+            src = po.at[piece, wrap(z + sign * turns(way, piece), Z)]
         else:
-            src = rs_out.at[way, half, step - 2]
+            src = rs_out.at[way, piece, step - 2]
         return send(
             src, rs_in.at[index], rs_s.at[index], rs_r.at[index], at(y, x, wrap(z + sign, Z), c)
         )
 
-    for half in range(2):
-        @pl.loop(0, Y // 2)
+    for piece in range(PIECES):
+        @pl.loop(0, Y // PIECES)
         def _(j):
-            block = half * (Y // 2) + j
+            block = piece * (Y // PIECES) + j
             sums = jnp.dot(
                 w_all[0:X].reshape(256, COLS), dd[0, block], preferred_element_type=F32
             ) + jnp.dot(w_all[X:].reshape(256, COLS), dd[1, block], preferred_element_type=F32)
             sums = sums.reshape(X, Z, 8, BLOCK)
             columns = pl.ds(pl.multiple_of(j * BLOCK, BLOCK), BLOCK)
             for k in range(Z):
-                po[half, k, :, columns] = sums[:, k].reshape(X * 8, BLOCK).astype(BF16)
+                po[piece, k, :, columns] = sums[:, k].reshape(X * 8, BLOCK).astype(BF16)
 
         for way in range(2):
-            rs(way, half, 1).start()
-
-    def finish(half):
-        sums = po[half, z].astype(F32)
+            rs(way, piece, 1).start()
+
+    def finish(piece):
+        sums = po[piece, z].astype(F32)
         for way in range(2):
-            sums = sums + rs_in[way, half, hops(way, half) - 1].astype(F32)
+            sums = sums + rs_in[way, piece, turns(way, piece) - 1].astype(F32)
         for k in range(X):
             lines = sums[k * 8 : k * 8 + 8]
-            lines = jnp.concatenate([lines[:, :1024], lines[:, 1024:]], axis=0)
-            fin_send[half, k] = lines.astype(BF16)
+            lines = jnp.concatenate([lines[:, : PIECE // 2], lines[:, PIECE // 2 :]], axis=0)
+            fin_send[piece, k] = lines.astype(BF16)
         for k in (2, 1, 3):
             target = wrap(x + k, X)
             send(
-                fin_send.at[half, target], fin_in.at[half, x], fin_s.at[half], fin_r.at[half],
+                fin_send.at[piece, target], fin_in.at[piece, x], fin_s.at[piece], fin_r.at[piece],
                 at(y, target, z, c),
             ).start()
-        fin_in[half, x] = fin_send[half, x]
+        fin_in[piece, x] = fin_send[piece, x]
 
     flush()
     for step in range(1, 5):
-        for half in range(2):
+        for piece in range(PIECES):
             for way in range(2):
-                if step > hops(way, half):
+                if step > turns(way, piece):
                     continue
-                rs(way, half, step).wait_recv()
-                if step < hops(way, half):
-                    target = wrap(z + (1 - 2 * way) * (hops(way, half) - step), Z)
-                    rs_out[way, half, step - 1] = (
-                        rs_in[way, half, step - 1].astype(F32) + po[half, target].astype(F32)
+                rs(way, piece, step).wait_recv()
+                if step < turns(way, piece):
+                    target = wrap(z + (1 - 2 * way) * (turns(way, piece) - step), Z)
+                    rs_out[way, piece, step - 1] = (
+                        rs_in[way, piece, step - 1].astype(F32) + po[piece, target].astype(F32)
                     ).astype(BF16)
-                    rs(way, half, step + 1).start()
+                    rs(way, piece, step + 1).start()
             if step == 4:
-                finish(half)
+                finish(piece)
 
     def drain_rs():
-        for half in range(2):
+        for piece in range(PIECES):
             for way in range(2):
-                for step in range(1, hops(way, half) + 1):
-                    rs(way, half, step).wait_send()
+                for step in range(1, turns(way, piece) + 1):
+                    rs(way, piece, step).wait_send()
     drain_rs()
-    for half in range(2):
-        take(fin_in.at[half, pl.ds(0, X - 1)], fin_r.at[half])
+    for piece in range(PIECES):
+        take(fin_in.at[piece, pl.ds(0, X - 1)], fin_r.at[piece])
         for k in range(X):
-            lines = fin_in[half, k].astype(F32)
-            for quarter in range(2):
-                for part_block in range(2):
-                    block = half * 4 + quarter * 2 + part_block
-                    begin = (block * X + k) * BLOCK
-                    out_ref[:, begin : begin + BLOCK] = lines[
-                        quarter * 8 : quarter * 8 + 8, part_block * BLOCK : (part_block + 1) * BLOCK
-                    ].astype(BF16)
+            lines = fin_in[piece, k].astype(F32)
+            for part_block in range(Y // PIECES):
+                block = piece * (Y // PIECES) + part_block
+                begin = (block * X + k) * BLOCK
+                out_ref[:, begin : begin + BLOCK] = lines[
+                    part_block * 8 : part_block * 8 + 8
+                ].astype(BF16)
 
     def drain_fin():
-        for half in range(2):
-            take(fin_in.at[half, pl.ds(0, X - 1)], fin_s.at[half])
+        for piece in range(PIECES):
+            take(fin_in.at[piece, pl.ds(0, X - 1)], fin_s.at[piece])
     drains.append(drain_fin)
     flush()
 
@@ -453,17 +458,17 @@
             pltpu.VMEM((2, Z * 8, COLS), BF16),
             pltpu.VMEM((2 * X, Z * 8, COLS), BF16),
             pltpu.VMEM((1, X * N_COL, 2, ROWS), F32),
-            pltpu.VMEM((2, Z, X * 8, 2048), BF16),
-            pltpu.VMEM((2, 2, 4, X * 8, 2048), BF16),
-            pltpu.VMEM((2, 2, 3, X * 8, 2048), BF16),
-            pltpu.VMEM((2, X, 16, 1024), BF16),
-            pltpu.VMEM((2, X, 16, 1024), BF16),
+            pltpu.VMEM((PIECES, Z, X * 8, PIECE), BF16),
+            pltpu.VMEM((2, PIECES, 4, X * 8, PIECE), BF16),
+            pltpu.VMEM((2, PIECES, 3, X * 8, PIECE), BF16),
+            pltpu.VMEM((PIECES, X, 16, PIECE // 2), BF16),
+            pltpu.VMEM((PIECES, X, 16, PIECE // 2), BF16),
             dma((2, CHUNKS // 2)), dma((2, CHUNKS // 2)),
             dma((2,)), dma((2, 2, CHUNKS, 4)),
             dma, dma((2, CHUNKS, 5)), dma, dma,
             dma((3,)), dma((3,)), dma, dma,
             dma((ITERS,)), dma((ITERS,)), dma((ITERS,)), dma((ITERS,)), dma, dma, dma((1,)), dma((1,)),
-            dma((2, 2, 4)), dma((2, 2, 4)), dma((2,)), dma((2,)),
+            dma((2, PIECES, 4)), dma((2, PIECES, 4)), dma((PIECES,)), dma((PIECES,)),
         ],
         compiler_params=pltpu.CompilerParams(
             collective_id=0, has_side_effects=True, vmem_limit_bytes=60 * 2**20

time: 124 us -> 122 us (0.984)
  Pallas kernels: 120 us -> 118 us
    pallas_call x1, Pallas kernels: 120 us -> 118 us  [per_device(): pl.pallas_call(kernel, out_shape=(jax.ShapeDtypeStruct((8, LATENT), BF16)...]
where the time goes in v5:
time: 122 us
  Pallas kernels  118 us (97%)
  local copies, waits for them, and re-layouts  2.91 us (2%)
    pallas_call x1, Pallas kernels, per_device(): pl.pallas_call(kernel, out_shape=(jax.ShapeDtypeStruct((8, LATENT), BF16)...  118 us
    unnamed x7, local copies, waits for them, and re-layouts  2.91 us

profile of v5, /device:TPU:8, one launch (start us, length us, event | category | flops | bytes accessed | tf_op | source)
XLA Modules:
  0.0 122.0 jit_solution(16499962342248550777)
XLA Ops:
  0.6 118.4 %coupling.1 = (bf16[8,16384]{1,0:T(8,128)(2,1)}, f32[1,128]{1,0:T(1,128)}, f32[1,256]{1,0:T(1,128)}) custom-call(bf16[128,1024]{1,0:T(8,128)(2,1)} %noise_hbm.1, bf16[256,512]{1,0:T(8,128)(2,1)} %data_hbm.1), custom_call_target="tpu_custom_call" | custom-call | tf_op jit(solution)/shard_map/coupling/pallas_call | solution.py:437
  119.0 0.0 copy-start.1
  119.1 1.7 %copy.8 = bf16[8,16384]{1,0:T(8,128)(2,1)} copy(bf16[8,16384]{1,0:T(8,128)(2,1)} %get-tuple-element.12) | data formatting | bytes 524288
  120.7 0.0 copy-done.1
  120.7 0.0 copy-start
  120.7 0.5 copy.9
  121.2 0.2 copy-done
  121.4 0.6 copy.10
Async XLA Ops:
  119.0 1.7 %copy-start.1 = (f32[1,128]{1,0:T(1,128)S(1)}, f32[1,128]{1,0:T(1,128)}, u32[]{:S(2)}) copy-start(f32[1,128]{1,0:T(1,128)} %get-tuple-element.7) | copy-start | bytes 1540
  120.7 0.7 copy-start

commit v6 on v5

--- a/solution.py
+++ b/solution.py
@@ -79,6 +79,12 @@
         while drains:
             drains.pop(0)()
 
+    data_ref = dd.at[c, y]
+    noise_in = pltpu.make_async_copy(noise_hbm, noise_ref, in_sem.at[0])
+    data_in = pltpu.make_async_copy(data_hbm, data_ref, in_sem.at[1])
+    noise_in.start()
+    data_in.start()
+
     barrier = pltpu.get_barrier_semaphore()
     near = [at(wrap(y + 1, Y), x, z, c), at(wrap(y - 1, Y), x, z, c)]
     near += [at(y, x, wrap(z + 1, Z), c), at(y, x, wrap(z - 1, Z), c), at(y, x, z, other)]
@@ -86,11 +92,6 @@
         near += [at(y, wrap(x + k, X), z, c), at(y, wrap(x + k, X), z, other)]
     for device in near:
         pl.semaphore_signal(barrier, inc=1, device_id=device, device_id_type=MESH)
-    data_ref = dd.at[c, y]
-    noise_in = pltpu.make_async_copy(noise_hbm, noise_ref, in_sem.at[0])
-    data_in = pltpu.make_async_copy(data_hbm, data_ref, in_sem.at[1])
-    noise_in.start()
-    data_in.start()
     part[...] = jnp.zeros_like(part)
     noise_in.wait()
     data_in.wait()
@@ -417,11 +418,11 @@
         take(fin_in.at[piece, pl.ds(0, X - 1)], fin_r.at[piece])
         for k in range(X):
             lines = fin_in[piece, k].astype(F32)
-            for part_block in range(Y // PIECES):
-                block = piece * (Y // PIECES) + part_block
-                begin = (block * X + k) * BLOCK
-                out_ref[:, begin : begin + BLOCK] = lines[
-                    part_block * 8 : part_block * 8 + 8
+            for part_piece in range(2):
+                block, inner = divmod(piece * PIECE + part_piece * (PIECE // 2), BLOCK)
+                begin = (block * X + k) * BLOCK + inner
+                out_ref[:, begin : begin + PIECE // 2] = lines[
+                    part_piece * 8 : part_piece * 8 + 8
                 ].astype(BF16)
 
     def drain_fin():
@@ -471,7 +472,7 @@
             dma((2, PIECES, 4)), dma((2, PIECES, 4)), dma((PIECES,)), dma((PIECES,)),
         ],
         compiler_params=pltpu.CompilerParams(
-            collective_id=0, has_side_effects=True, vmem_limit_bytes=60 * 2**20
+            collective_id=0, has_side_effects=True, vmem_limit_bytes=107 * 2**19
         ),
         name="coupling",
     )(noise, data)

time: 122 us -> 120 us (0.984)
    unnamed x7 -> x3, local copies, waits for them, and re-layouts: 2.91 us -> 1.78 us
where the time goes in v6:
time: 120 us
  Pallas kernels  118 us (98%)
  local copies, waits for them, and re-layouts  1.78 us (1%)
    pallas_call x1, Pallas kernels, per_device(): pl.pallas_call(kernel, out_shape=(jax.ShapeDtypeStruct((8, LATENT), BF16)...  118 us

profile of v6, /device:TPU:8, one launch (start us, length us, event | category | flops | bytes accessed | tf_op | source)
XLA Modules:
  0.0 120.1 jit_solution(13731947991348257802)
XLA Ops:
  0.6 117.7 %coupling.1 = (bf16[8,16384]{1,0:T(8,128)(2,1)S(1)}, f32[1,128]{1,0:T(1,128)S(1)}, f32[1,256]{1,0:T(1,128)S(1)}) custom-call(bf16[128,1024]{1,0:T(8,128)(2,1)} %noise_hbm.1, bf16[256,512]{1,0:T(8,128)(2,1)} %data_hbm.1), custom_call_target="tpu_custom_call" | custom-call | tf_op jit(solution)/shard_map/coupling/pallas_call | solution.py:438
  118.4 0.7 copy.8
  119.1 0.5 copy.9
  119.6 0.6 copy.10

commit v7 on v6

--- a/solution.py
+++ b/solution.py
@@ -231,8 +231,9 @@
         copy.wait_recv()
     total = part[pl.ds(pl.multiple_of(x * ROWS, ROWS), ROWS), :]
     total = total + part_in[0] + part_in[1] + part_in[2]
-    score[...] = total * (2.0 / LATENT / EPSILON)
-    score_t[...] = jnp.transpose(score[...])
+    total = total * (2.0 / LATENT / EPSILON)
+    score_t[...] = jnp.transpose(total)
+    score[...] = total
     take(norm_slots.at[pl.ds(0, X - 1)], norm_r)
     data_norm = (norm_slots[0] + norm_slots[1] + norm_slots[2] + norm_slots[3]) / LATENT
 

time: 120 us -> 120 us (level)
  no operation moved by 1% of the time
where the time goes in v7:
time: 120 us
  Pallas kernels  118 us (98%)
  local copies, waits for them, and re-layouts  1.78 us (1%)
    pallas_call x1, Pallas kernels, per_device(): pl.pallas_call(kernel, out_shape=(jax.ShapeDtypeStruct((8, LATENT), BF16)...  118 us

profile of v7, /device:TPU:8, one launch (start us, length us, event | category | flops | bytes accessed | tf_op | source)
XLA Modules:
  0.0 120.1 jit_solution(13731947991348257802)
XLA Ops:
  0.6 117.7 %coupling.1 = (bf16[8,16384]{1,0:T(8,128)(2,1)S(1)}, f32[1,128]{1,0:T(1,128)S(1)}, f32[1,256]{1,0:T(1,128)S(1)}) custom-call(bf16[128,1024]{1,0:T(8,128)(2,1)} %noise_hbm.1, bf16[256,512]{1,0:T(8,128)(2,1)} %data_hbm.1), custom_call_target="tpu_custom_call" | custom-call | tf_op jit(solution)/shard_map/coupling/pallas_call | solution.py:439
  118.4 0.7 copy.8
  119.1 0.5 copy.9
  119.6 0.6 copy.10
